TPU v7x, 32 devices: a whole 2x2x4 slice. The times are simulated.
32 devices in a mesh: train: 8 (over z, y), tile: 4 (over x, core).
Axes of the slice: x: 2, y: 2, z: 4, core: 2. Of those that a mesh axis runs over, the one named last changes fastest.
Arguments:
- test_grads: bfloat16 [1024, 4096], P('train', 'tile'), may hold values from -6 to 6
- fisher: bfloat16 [8, 512, 512], P('tile'), may hold values from -8 to 8
- train_grads: bfloat16 [32768, 4096], P(('train', 'tile')), may hold values from -0.09375 to 0.09375
- candidates: int32 [1024, 4], P('train'), may hold values from 0 to 7, all different within a row; in each aligned block of 128 rows (0 to 127, 128 to 255, ...) at most 96 rows name the same one
- shard_rows: int32 [8], P('train'), may hold values from 1024 to 4096
Outputs:
- top_scores: float32 [1024, 32], P('train')
Inputs may be any that keep to these rules, and one draw needn't show every extreme that they name: `candidates`: each row names 4 different shards; among the rows of one index of train no shard is named by more than 96 rows.
All inputs are finite; a program needn't handle non-finite values.
Results may differ from a plain program's by a relative error of at most 0.0011.
Values may be sent and summed in bfloat16 or wider, within the bound.
A program may use at most 128 MiB of HBM per device.

v0:
```python
import functools

import jax
import jax.numpy as jnp
from jax import lax
from jax.experimental import pallas as pl
from jax.experimental.pallas import tpu as pltpu
from jax.sharding import PartitionSpec as P

TOPK = 32
MESH = pl.DeviceIdType.MESH

lowest_score = -1e30


def combined_all(part, axis, combine):
    gathered = lax.all_gather(part, axis)

    def take(source):
        return lax.dynamic_index_in_dim(gathered, source, 0, False)

    return lax.fori_loop(
        1, lax.axis_size(axis), lambda source, state: combine(state, take(source)), take(0)
    )


def combine_leaders(earlier_best, later_best):
    joined = jnp.concatenate([earlier_best, later_best], axis=-1)
    return lax.top_k(joined, earlier_best.shape[-1])[0]


def shards(test_grads, fisher, train_grads, candidates, shard_rows):
    train_count = lax.axis_size("train")
    q_rows, columns = test_grads.shape
    blocks, block_order, _ = fisher.shape
    cand_count = candidates.shape[1]
    local_rows = train_grads.shape[0]
    capacity = max(2, 3 * q_rows * cand_count // (2 * train_count))
    precond = jnp.einsum(
        "qbi,bij->qbj",
        test_grads.reshape(q_rows, blocks, block_order),
        fisher,
        preferred_element_type=jnp.float32,
    )
    precond = precond.reshape(q_rows, columns).astype(jnp.bfloat16)
    targets = candidates.reshape(-1)
    one_hot = (targets[:, None] == jnp.arange(train_count, dtype=jnp.int32)[None, :]).astype(
        jnp.int32
    )
    earlier = jnp.cumsum(one_hot, axis=0) - one_hot
    rank_in = jnp.sum(earlier * one_hot, axis=1)
    slot_index = targets * capacity + rank_in
    sources = jnp.arange(q_rows * cand_count, dtype=jnp.int32) // cand_count
    owner_row = jnp.full((train_count * capacity,), q_rows, jnp.int32).at[slot_index].set(sources)
    row_ids = lax.axis_index("tile") * local_rows + jnp.arange(local_rows, dtype=jnp.int32)
    alive_rows = row_ids < shard_rows[0]
    complete = lax.all_gather(precond, "tile", axis=1, tiled=True)
    padded = jnp.concatenate([complete, jnp.zeros((1, complete.shape[1]), jnp.bfloat16)], axis=0)
    outgoing = padded[owner_row].reshape(train_count, capacity, complete.shape[1])
    scores = jnp.einsum(
        "nck,rk->ncr",
        lax.all_to_all(outgoing, "train", split_axis=0, concat_axis=0, tiled=True),
        train_grads,
        preferred_element_type=jnp.float32,
    )
    masked = jnp.where(alive_rows, scores, lowest_score)
    leaders = lax.top_k(masked, TOPK)[0]
    leaders = combined_all(leaders, "tile", combine_leaders)
    returned = lax.all_to_all(leaders, "train", split_axis=0, concat_axis=0, tiled=True)
    flattened = returned.reshape(train_count * capacity, TOPK)
    per_pair = flattened[slot_index].reshape(q_rows, cand_count * TOPK)
    result_best = lax.top_k(per_pair, TOPK)[0]
    return result_best


def batcher(n):
    pairs = []
    p = 1
    while p < n:
        k = p
        while k >= 1:
            for j in range(k % p, n - k, 2 * k):
                for i in range(min(k, n - j - k)):
                    if (i + j) // (2 * p) == (i + j + k) // (2 * p):
                        pairs.append((i + j, i + j + k))
            k //= 2
        p *= 2
    return pairs


def sort_down(values):
    values = list(values)
    for i, j in batcher(len(values)):
        a, b = values[i], values[j]
        values[i], values[j] = jnp.maximum(a, b), jnp.minimum(a, b)
    return values


def merge_top(first, second):
    n = len(first)
    values = [jnp.maximum(first[i], second[n - 1 - i]) for i in range(n)]
    d = n // 2
    while d >= 1:
        for i in range(n):
            if not i & d:
                a, b = values[i], values[i + d]
                values[i], values[i + d] = jnp.maximum(a, b), jnp.minimum(a, b)
        d //= 2
    return values


def over_sublanes(values):
    for shift in (4, 2, 1):
        values = merge_top(values, [pltpu.roll(v, shift, 0) for v in values])
    return values


def kernel(
    test_hbm, fisher_hbm, train_hbm, cand_hbm, rows_ref, out_ref,
    test, fisher, train, cand, gathered, acc, best, sent, homed, tiles,
    send_sem, recv_sem, load_sem,
):
    me, tile = lax.axis_index("train"), lax.axis_index("tile")
    z, y = me // 2, me % 2
    x, core = tile // 2, tile % 2
    q, width = test.shape
    half = q // 2
    order = fisher.shape[1]
    local_rows = train.shape[0]

    inner = (z == 1) | (z == 2)
    outer = (z == 0) | (z == 3)
    flag = ((z + 1) // 2) % 2
    across, two_on = 3 - z, (z + 2) % 4
    zs = [
        z,
        z + 1 - 2 * (z % 2),
        two_on + flag * (across - two_on),
        across + flag * (two_on - across),
    ]
    ys = [y, 1 - y]
    at_tile = [tile, x * 2 + 1 - core, (1 - x) * 2 + core, (1 - x) * 2 + 1 - core]

    def home(a, yr):
        return (zs[a] * 2 + ys[yr], tile)

    def at(t):
        return (me, at_tile[t])

    loads = [
        pltpu.make_async_copy(test_hbm, test, load_sem.at[0]),
        pltpu.make_async_copy(fisher_hbm, fisher, load_sem.at[1]),
        pltpu.make_async_copy(cand_hbm, cand, load_sem.at[2]),
    ]
    for t in range(4):
        start = pl.multiple_of(at_tile[t] * width, width)
        loads.append(pltpu.make_async_copy(
            train_hbm.at[:, pl.ds(start, width)],
            train.at[:, pl.ds(t * width, width)],
            load_sem.at[3 + t],
        ))
    for load in loads:
        load.start()
    barrier = pltpu.get_barrier_semaphore()
    peers = [home(a, yr) for a in range(4) for yr in range(2) if a or yr]
    peers += [at(t) for t in range(1, 4)]
    for peer in peers:
        pl.semaphore_signal(barrier, inc=1, device_id=peer, device_id_type=MESH)

    homed[...] = jnp.full_like(homed, lowest_score)
    tiles[...] = jnp.full_like(tiles, lowest_score)
    loads[0].wait()
    loads[1].wait()
    for b in range(fisher.shape[0]):
        columns = slice(b * order, (b + 1) * order)
        gathered[0, :q, columns] = jnp.dot(
            test[:, columns], fisher[b], preferred_element_type=jnp.float32
        ).astype(jnp.bfloat16)
    pl.semaphore_wait(barrier, len(peers))

    copies = {}

    def copy_to(n, got, source, target, device):
        return pltpu.make_async_remote_copy(
            src_ref=source, dst_ref=target, send_sem=send_sem.at[n], recv_sem=recv_sem.at[got],
            device_id=device, device_id_type=MESH,
        )

    def send(name, source, target, device):
        n = len(copies) + 8
        copies[name] = copy_to(n, n, source, target, device)
        copies[name].start()

    def rows(a, t, start, count):
        return gathered.at[a, pl.ds(start, count), pl.ds(t * width, width)]

    def unit(a):
        return rows(a, 0, 0, q)

    to_pair = copy_to(0, 1, unit(0), unit(1), home(1, 0))
    inner_copies = [
        copy_to(1, 2, unit(0), unit(2), (across * 2 + y, tile)),
        copy_to(2, 3, unit(1), unit(3), (across * 2 + y, tile)),
        copy_to(3, 2, unit(2), unit(2), home(1, 0)),
        copy_to(4, 3, unit(3), unit(3), home(1, 0)),
    ]

    def arrived(a):
        copy_to(0, a, unit(0), unit(a), home(1, 0)).wait_recv()

    def first(a):
        send(("y", a), rows(a, 0, 0, q), rows(a, 0, q, q), home(0, 1))
        send(("x", a), rows(a, 0, 0, q), rows(a, 2, 0, q), at(2))
        send(("s00", a), rows(a, 0, 0, q), rows(a, 1, 0, q), at(1))

    def second(a):
        copies["y", a].wait_recv()
        send(("x2", a), rows(a, 0, q, half), rows(a, 2, q, half), at(2))
        copies["x", a].wait_recv()
        send(("y2", a), rows(a, 2, half, half), rows(a, 2, q + half, half), home(0, 1))
        send(("s10", a), rows(a, 0, q, q), rows(a, 1, q, q), at(1))
        send(("s01", a), rows(a, 2, 0, q), rows(a, 3, 0, q), at(1))

    def third(a):
        copies["x2", a].wait_recv()
        copies["y2", a].wait_recv()
        send(("s11", a), rows(a, 2, q, q), rows(a, 3, q, q), at(1))
        for name in ("s00", "s10", "s01", "s11"):
            copies[name, a].wait_recv()

    def compute(a):
        part_rows = local_rows // 2

        def multiply(r, carry):
            start = pl.multiple_of(r * part_rows, part_rows)
            part = lax.dot_general(
                train[pl.ds(start, part_rows), :], gathered[a],
                (((1,), (1,)), ((), ())), preferred_element_type=jnp.float32,
            )
            for g in range(2):
                acc[g, pl.ds(start, part_rows), :] = part[:, g * q:(g + 1) * q]
            return carry

        lax.fori_loop(0, 2, multiply, 0)

        live = rows_ref[0] - tile * local_rows
        step = 8 * TOPK

        def lanes(g, carry):
            best[...] = jnp.full_like(best, lowest_score)

            def block(j, carry):
                base = pl.multiple_of(j * step, step)
                ids = lax.broadcasted_iota(jnp.int32, (8, q), 0) + base
                values = []
                for i in range(TOPK):
                    value = acc[g, pl.ds(base + 8 * i, 8), :]
                    values.append(jnp.where(ids + 8 * i < live, value, lowest_score))
                merged = merge_top([best[i] for i in range(TOPK)], sort_down(values))
                for i in range(TOPK):
                    best[i] = merged[i]
                return carry

            lax.fori_loop(0, local_rows // step, block, 0)
            merged = over_sublanes([best[i] for i in range(TOPK)])
            for i in range(TOPK):
                sent[a, g, i:i + 1, :] = merged[i][0:1]
            return carry

        lax.fori_loop(0, 2, lanes, 0)
        for yr in range(2):
            if a or yr:
                n = len(copies) + 8
                copies["h", a, yr] = copy_to(
                    n, 52 + me, sent.at[a, yr], homed.at[pl.ds(me * TOPK, TOPK)], home(a, yr)
                )
                copies["h", a, yr].start()
            else:
                homed[pl.ds(pl.multiple_of(me * TOPK, TOPK), TOPK)] = sent[0, 0]

    to_pair.start()

    @pl.when(inner)
    def _():
        inner_copies[0].start()

    first(0)
    arrived(1)

    @pl.when(inner)
    def _():
        inner_copies[1].start()
        arrived(2)
        inner_copies[2].start()

    first(1)
    second(0)

    @pl.when(inner)
    def _():
        arrived(3)
        inner_copies[3].start()

    @pl.when(outer)
    def _():
        arrived(2)

    first(2)
    third(0)
    for load in loads[2:]:
        load.wait()
    compute(0)
    second(1)

    @pl.when(outer)
    def _():
        arrived(3)

    first(3)
    third(1)
    compute(1)
    second(2)
    second(3)
    third(2)
    compute(2)
    third(3)
    compute(3)

    for d in range(1, 8):
        source = (me + d) % 8
        copy_to(
            0, 52 + source, sent.at[0, 0], homed.at[pl.ds(source * TOPK, TOPK)], home(0, 1)
        ).wait_recv()
    shard = lax.broadcasted_iota(jnp.int32, (8, q), 0)
    named = shard == cand[0:1, :]
    for c in range(1, cand.shape[0]):
        named = named | (shard == cand[c:c + 1, :])
    merged = over_sublanes([
        jnp.where(named, homed[pl.ds(i, 8, stride=TOPK), :], lowest_score) for i in range(TOPK)
    ])
    for i in range(TOPK):
        tiles[i:i + 1, :] = merged[i][0:1]
    for t in range(1, 4):
        send(("t", t), tiles.at[pl.ds(0, TOPK)], tiles.at[pl.ds(t * TOPK, TOPK)], at(t))
    for t in range(1, 4):
        copies["t", t].wait_recv()
    merged = over_sublanes([tiles[pl.ds(i, 8, stride=TOPK), :] for i in range(TOPK)])
    for i in range(TOPK):
        out_ref[i:i + 1, :] = merged[i][0:1]
    for copy in copies.values():
        copy.wait_send()
    to_pair.wait_send()

    @pl.when(inner)
    def _():
        for copy in inner_copies:
            copy.wait_send()


def fused(test_grads, fisher, train_grads, candidates, shard_rows):
    q, width = test_grads.shape
    local_rows, columns = train_grads.shape
    anywhere = pl.BlockSpec(memory_space=pl.ANY)
    best = pl.pallas_call(
        kernel,
        out_shape=jax.ShapeDtypeStruct((TOPK, q), jnp.float32),
        in_specs=[anywhere] * 4 + [pl.BlockSpec(memory_space=pltpu.SMEM)],
        out_specs=pl.BlockSpec(memory_space=pltpu.VMEM),
        scratch_shapes=[
            pltpu.VMEM(test_grads.shape, jnp.bfloat16),
            pltpu.VMEM(fisher.shape, jnp.bfloat16),
            pltpu.VMEM((local_rows, columns), jnp.bfloat16),
            pltpu.VMEM(candidates.shape[::-1], jnp.int32),
            pltpu.VMEM((4, 2 * q, columns), jnp.bfloat16),
            pltpu.VMEM((2, local_rows, q), jnp.float32),
            pltpu.VMEM((TOPK, 8, q), jnp.float32),
            pltpu.VMEM((4, 2, TOPK, q), jnp.float32),
            pltpu.VMEM((8 * TOPK, q), jnp.float32),
            pltpu.VMEM((8 * TOPK, q), jnp.float32),
            pltpu.SemaphoreType.DMA((60,)),
            pltpu.SemaphoreType.DMA((60,)),
            pltpu.SemaphoreType.DMA((7,)),
        ],
        compiler_params=pltpu.CompilerParams(
            collective_id=0, has_side_effects=True, vmem_limit_bytes=56 * 1024 * 1024
        ),
    )(test_grads, fisher, train_grads, candidates.T, shard_rows)
    return best.T


def solution(mesh):
    placed = (
        P("train", "tile"),
        P("tile", None, None),
        P(("train", "tile"), None),
        P("train", None),
        P("train"),
    )
    sizes = (mesh.shape["train"], mesh.shape["tile"])
    return jax.shard_map(
        fused if sizes == (8, 4) else shards,
        mesh=mesh, in_specs=placed, out_specs=P("train", None), check_vma=False,
    )
```

profile of v0, /device:TPU:0, one launch (start us, length us, event | category | flops | bytes accessed | tf_op | source)
XLA Modules:
  0.0 65.0 jit_solution(485375432331985459)
XLA Ops:
  0.7 63.0 %shard_map.55 = f32[32,128]{1,0:T(8,128)} custom-call(bf16[128,1024]{1,0:T(8,128)(2,1)} %test_hbm.1, bf16[2,512,512]{2,1,0:T(8,128)(2,1)} %fisher_hbm.1, bf16[1024,4096]{1,0:T(8,128)(2,1)} %train_hbm.1, s32[4,128]{1,0:T(4,128)} %bitcast.3, s32[1]{0:T(128)S(6)} %copy.7.rows_ref), custom_call_target="tpu_custom_call" | custom-call | tf_op jit(solution)/shard_map/pallas_call | solution.py:364
  63.7 1.3 %copy.8 = f32[128,32]{0,1:T(8,128)} copy(f32[128,32]{0,1:T(8,128)} %bitcast.2) | data formatting | bytes 32768
where the time goes:
time: 65.3 us; the launch traced here: 65 us
  Pallas kernels  63 us (96%)
  local copies, waits for them, and re-layouts  1.32 us (2%)
  between operations  0.66 us (1%)
    pallas_call x1, Pallas kernels, fused(): pl.pallas_call(kernel, out_shape=jax.ShapeDtypeStruct((TOPK, q), jnp.floa...  63 us
    unnamed x1, local copies, waits for them, and re-layouts  1.32 us

commit v1 on v0

--- a/solution.py
+++ b/solution.py
@@ -124,7 +124,10 @@
     z, y = me // 2, me % 2
     x, core = tile // 2, tile % 2
     q, width = test.shape
-    half = q // 2
+    plain, flat = 3 * q // 4, q // 4
+    half, flat_half = plain // 2, flat // 2
+    flats = 2 * plain
+    place = (0, 2, 1, 3)
     order = fisher.shape[1]
     local_rows = train.shape[0]
 
@@ -156,11 +159,11 @@
         start = pl.multiple_of(at_tile[t] * width, width)
         loads.append(pltpu.make_async_copy(
             train_hbm.at[:, pl.ds(start, width)],
-            train.at[:, pl.ds(t * width, width)],
+            train.at[:, pl.ds(place[t] * width, width)],
             load_sem.at[3 + t],
         ))
-    for load in loads:
-        load.start()
+    loads[0].start()
+    loads[1].start()
     barrier = pltpu.get_barrier_semaphore()
     peers = [home(a, yr) for a in range(4) for yr in range(2) if a or yr]
     peers += [at(t) for t in range(1, 4)]
@@ -171,11 +174,15 @@
     tiles[...] = jnp.full_like(tiles, lowest_score)
     loads[0].wait()
     loads[1].wait()
+    for load in loads[2:]:
+        load.start()
     for b in range(fisher.shape[0]):
         columns = slice(b * order, (b + 1) * order)
-        gathered[0, :q, columns] = jnp.dot(
+        done = jnp.dot(
             test[:, columns], fisher[b], preferred_element_type=jnp.float32
         ).astype(jnp.bfloat16)
+        gathered[0, :plain, columns] = done[:plain]
+        gathered[0, flats:flats + flat, columns] = done[plain:]
     pl.semaphore_wait(barrier, len(peers))
 
     copies = {}
@@ -187,45 +194,74 @@
         )
 
     def send(name, source, target, device):
-        n = len(copies) + 8
+        n = len(copies) + 10
         copies[name] = copy_to(n, n, source, target, device)
         copies[name].start()
 
     def rows(a, t, start, count):
-        return gathered.at[a, pl.ds(start, count), pl.ds(t * width, width)]
+        return gathered.at[a, pl.ds(start, count), pl.ds(place[t] * width, width)]
 
     def unit(a):
-        return rows(a, 0, 0, q)
-
-    to_pair = copy_to(0, 1, unit(0), unit(1), home(1, 0))
-    inner_copies = [
-        copy_to(1, 2, unit(0), unit(2), (across * 2 + y, tile)),
-        copy_to(2, 3, unit(1), unit(3), (across * 2 + y, tile)),
-        copy_to(3, 2, unit(2), unit(2), home(1, 0)),
-        copy_to(4, 3, unit(3), unit(3), home(1, 0)),
-    ]
+        return rows(a, 0, 0, plain)
+
+    def plane(a, cr=0):
+        return gathered.at[a, pl.ds(flats, 2 * flat), pl.ds(cr * 2 * width, 2 * width)]
+
+    def chain(part, base):
+        inner_home = (across * 2 + y, tile)
+        return [
+            copy_to(base, base + 1, part(0), part(1), home(1, 0)),
+            copy_to(base + 1, base + 2, part(0), part(2), inner_home),
+            copy_to(base + 2, base + 3, part(1), part(3), inner_home),
+            copy_to(base + 3, base + 2, part(2), part(2), home(1, 0)),
+            copy_to(base + 4, base + 3, part(3), part(3), home(1, 0)),
+        ]
+
+    units, planes = chain(unit, 0), chain(plane, 5)
 
     def arrived(a):
         copy_to(0, a, unit(0), unit(a), home(1, 0)).wait_recv()
 
+    def plane_arrived(a):
+        copy_to(5, 5 + a, plane(0), plane(a), home(1, 0)).wait_recv()
+
+    def plane_first():
+        send("cy", rows(0, 0, flats, flat), rows(0, 0, flats + flat, flat), home(0, 1))
+        send("cx", rows(0, 0, flats, flat), rows(0, 2, flats, flat), at(2))
+
+    def plane_second():
+        copies["cy"].wait_recv()
+        other = flats + flat
+        send("cx2", rows(0, 0, other, flat_half), rows(0, 2, other, flat_half), at(2))
+        copies["cx"].wait_recv()
+        send(
+            "cy2", rows(0, 2, flats + flat_half, flat_half),
+            rows(0, 2, other + flat_half, flat_half), home(0, 1),
+        )
+        copies["cx2"].wait_recv()
+        copies["cy2"].wait_recv()
+
+    def plane_over(a):
+        send(("cs", a), plane(a), plane(a, 1), at(1))
+
     def first(a):
-        send(("y", a), rows(a, 0, 0, q), rows(a, 0, q, q), home(0, 1))
-        send(("x", a), rows(a, 0, 0, q), rows(a, 2, 0, q), at(2))
-        send(("s00", a), rows(a, 0, 0, q), rows(a, 1, 0, q), at(1))
+        send(("y", a), rows(a, 0, 0, plain), rows(a, 0, plain, plain), home(0, 1))
+        send(("x", a), rows(a, 0, 0, plain), rows(a, 2, 0, plain), at(2))
+        send(("s00", a), rows(a, 0, 0, plain), rows(a, 1, 0, plain), at(1))
 
     def second(a):
         copies["y", a].wait_recv()
-        send(("x2", a), rows(a, 0, q, half), rows(a, 2, q, half), at(2))
+        send(("x2", a), rows(a, 0, plain, half), rows(a, 2, plain, half), at(2))
         copies["x", a].wait_recv()
-        send(("y2", a), rows(a, 2, half, half), rows(a, 2, q + half, half), home(0, 1))
-        send(("s10", a), rows(a, 0, q, q), rows(a, 1, q, q), at(1))
-        send(("s01", a), rows(a, 2, 0, q), rows(a, 3, 0, q), at(1))
+        send(("y2", a), rows(a, 2, half, half), rows(a, 2, plain + half, half), home(0, 1))
+        send(("s10", a), rows(a, 0, plain, plain), rows(a, 1, plain, plain), at(1))
+        send(("s01", a), rows(a, 2, 0, plain), rows(a, 3, 0, plain), at(1))
 
     def third(a):
         copies["x2", a].wait_recv()
         copies["y2", a].wait_recv()
-        send(("s11", a), rows(a, 2, q, q), rows(a, 3, q, q), at(1))
-        for name in ("s00", "s10", "s01", "s11"):
+        send(("s11", a), rows(a, 2, plain, plain), rows(a, 3, plain, plain), at(1))
+        for name in ("s00", "s10", "s01", "s11", "cs"):
             copies[name, a].wait_recv()
 
     def compute(a):
@@ -233,8 +269,12 @@
 
         def multiply(r, carry):
             start = pl.multiple_of(r * part_rows, part_rows)
+            chunk = jnp.concatenate([
+                gathered[a, :plain], gathered[a, flats:flats + flat],
+                gathered[a, plain:flats], gathered[a, flats + flat:],
+            ], axis=0)
             part = lax.dot_general(
-                train[pl.ds(start, part_rows), :], gathered[a],
+                train[pl.ds(start, part_rows), :], chunk,
                 (((1,), (1,)), ((), ())), preferred_element_type=jnp.float32,
             )
             for g in range(2):
@@ -270,28 +310,37 @@
         lax.fori_loop(0, 2, lanes, 0)
         for yr in range(2):
             if a or yr:
-                n = len(copies) + 8
+                n = len(copies) + 10
                 copies["h", a, yr] = copy_to(
-                    n, 52 + me, sent.at[a, yr], homed.at[pl.ds(me * TOPK, TOPK)], home(a, yr)
+                    n, 60 + me, sent.at[a, yr], homed.at[pl.ds(me * TOPK, TOPK)], home(a, yr)
                 )
                 copies["h", a, yr].start()
             else:
                 homed[pl.ds(pl.multiple_of(me * TOPK, TOPK), TOPK)] = sent[0, 0]
 
-    to_pair.start()
-
-    @pl.when(inner)
-    def _():
-        inner_copies[0].start()
+    plane_first()
+    units[0].start()
+
+    @pl.when(inner)
+    def _():
+        units[1].start()
 
     first(0)
+    plane_second()
+    planes[0].start()
+
+    @pl.when(inner)
+    def _():
+        planes[1].start()
+
+    plane_over(0)
     arrived(1)
 
     @pl.when(inner)
     def _():
-        inner_copies[1].start()
+        units[2].start()
         arrived(2)
-        inner_copies[2].start()
+        units[3].start()
 
     first(1)
     second(0)
@@ -299,7 +348,16 @@
     @pl.when(inner)
     def _():
         arrived(3)
-        inner_copies[3].start()
+        units[4].start()
+
+    plane_arrived(1)
+    plane_over(1)
+
+    @pl.when(inner)
+    def _():
+        planes[2].start()
+        plane_arrived(2)
+        planes[3].start()
 
     @pl.when(outer)
     def _():
@@ -312,6 +370,11 @@
     compute(0)
     second(1)
 
+    @pl.when(inner)
+    def _():
+        plane_arrived(3)
+        planes[4].start()
+
     @pl.when(outer)
     def _():
         arrived(3)
@@ -320,16 +383,28 @@
     third(1)
     compute(1)
     second(2)
+
+    @pl.when(outer)
+    def _():
+        plane_arrived(2)
+
+    plane_over(2)
     second(3)
     third(2)
     compute(2)
+
+    @pl.when(outer)
+    def _():
+        plane_arrived(3)
+
+    plane_over(3)
     third(3)
     compute(3)
 
     for d in range(1, 8):
         source = (me + d) % 8
         copy_to(
-            0, 52 + source, sent.at[0, 0], homed.at[pl.ds(source * TOPK, TOPK)], home(0, 1)
+            0, 60 + source, sent.at[0, 0], homed.at[pl.ds(source * TOPK, TOPK)], home(0, 1)
         ).wait_recv()
     shard = lax.broadcasted_iota(jnp.int32, (8, q), 0)
     named = shard == cand[0:1, :]
@@ -349,22 +424,23 @@
         out_ref[i:i + 1, :] = merged[i][0:1]
     for copy in copies.values():
         copy.wait_send()
-    to_pair.wait_send()
-
-    @pl.when(inner)
-    def _():
-        for copy in inner_copies:
+    units[0].wait_send()
+    planes[0].wait_send()
+
+    @pl.when(inner)
+    def _():
+        for copy in units[1:] + planes[1:]:
             copy.wait_send()
 
 
 def fused(test_grads, fisher, train_grads, candidates, shard_rows):
     q, width = test_grads.shape
     local_rows, columns = train_grads.shape
-    anywhere = pl.BlockSpec(memory_space=pl.ANY)
+    far = pl.BlockSpec(memory_space=pl.ANY)
     best = pl.pallas_call(
         kernel,
         out_shape=jax.ShapeDtypeStruct((TOPK, q), jnp.float32),
-        in_specs=[anywhere] * 4 + [pl.BlockSpec(memory_space=pltpu.SMEM)],
+        in_specs=[far] * 4 + [pl.BlockSpec(memory_space=pltpu.SMEM)],
         out_specs=pl.BlockSpec(memory_space=pltpu.VMEM),
         scratch_shapes=[
             pltpu.VMEM(test_grads.shape, jnp.bfloat16),
@@ -377,8 +453,8 @@
             pltpu.VMEM((4, 2, TOPK, q), jnp.float32),
             pltpu.VMEM((8 * TOPK, q), jnp.float32),
             pltpu.VMEM((8 * TOPK, q), jnp.float32),
-            pltpu.SemaphoreType.DMA((60,)),
-            pltpu.SemaphoreType.DMA((60,)),
+            pltpu.SemaphoreType.DMA((68,)),
+            pltpu.SemaphoreType.DMA((68,)),
             pltpu.SemaphoreType.DMA((7,)),
         ],
         compiler_params=pltpu.CompilerParams(

time: 65.3 us -> 63.9 us (0.979)
  Pallas kernels: 63 us -> 61.7 us
    pallas_call x1, Pallas kernels: 63 us -> 61.7 us  [fused(): pl.pallas_call(kernel, out_shape=jax.ShapeDtypeStruct((TOPK, q), jnp.floa...]
where the time goes in v1:
time: 63.9 us; the launch traced here: 63.7 us
  Pallas kernels  61.7 us (97%)
  local copies, waits for them, and re-layouts  1.32 us (2%)
  between operations  0.66 us (1%)
    pallas_call x1, Pallas kernels, fused(): pl.pallas_call(kernel, out_shape=jax.ShapeDtypeStruct((TOPK, q), jnp.floa...  61.7 us
    unnamed x1, local copies, waits for them, and re-layouts  1.32 us

profile of v1, /device:TPU:0, one launch (start us, length us, event | category | flops | bytes accessed | tf_op | source)
XLA Modules:
  0.0 63.7 jit_solution(12724652812327291784)
XLA Ops:
  0.7 61.7 %shard_map.55 = f32[32,128]{1,0:T(8,128)} custom-call(bf16[128,1024]{1,0:T(8,128)(2,1)} %test_hbm.1, bf16[2,512,512]{2,1,0:T(8,128)(2,1)} %fisher_hbm.1, bf16[1024,4096]{1,0:T(8,128)(2,1)} %train_hbm.1, s32[4,128]{1,0:T(4,128)} %bitcast.3, s32[1]{0:T(128)S(6)} %copy.7.rows_ref), custom_call_target="tpu_custom_call" | custom-call | tf_op jit(solution)/shard_map/pallas_call | solution.py:440
  62.3 1.3 %copy.8 = f32[128,32]{0,1:T(8,128)} copy(f32[128,32]{0,1:T(8,128)} %bitcast.2) | data formatting | bytes 32768
